TPU v7x, 128 devices: a whole 4x4x4 slice. The times are simulated.
128 devices in a mesh: batch: 64 (over z, y, x), feat: 2 (over core).
Axes of the slice: x: 4, y: 4, z: 4, core: 2. Of those that a mesh axis runs over, the one named last changes fastest.
Arguments:
- feature_store: bfloat16 [128, 1048576], P('feat', 'batch'), may hold values from -6 to 6
- requests: int32 [4096, 512], P('batch'), may hold values from 0 to 16383
- block_index: int32 [4096, 8], P('batch'), may hold values from 0 to 511, as said below
- block_values: bfloat16 [4096, 64, 512], P('batch'), may hold values from 0.049804688 to 1
- frontier: int32 [64], P('batch'), may hold values from 1 to 64, as said below
- self_first: bfloat16 [128, 256], replicated, may hold values from -0.5 to 0.5
- neigh_first: bfloat16 [128, 256], replicated, may hold values from -1.1953125 to 1.1953125
- bias_first: float32 [256], replicated, may hold values from -3 to 3
- second_index: int32 [4096, 8], P(('batch', 'feat')), may hold values from 0 to 63
- second_values: bfloat16 [4096, 64, 512], P(('batch', 'feat')), may hold values from 0.049804688 to 1
- self_second: bfloat16 [256, 256], replicated, may hold values from -0.375 to 0.375
- neigh_second: bfloat16 [256, 256], replicated, may hold values from -0.375 to 0.375
- bias_second: float32 [256], replicated, may hold values from -3 to 3
- classifier: bfloat16 [256, 172], replicated, may hold values from -0.375 to 0.375
- bias_class: float32 [172], replicated, may hold values from -3 to 3
Outputs:
- logits: float32 [262144, 172], P(('batch', 'feat'))
Inputs may be any that keep to these rules, and one draw needn't show every extreme that they name: `frontier`: exactly one batch group has all 64 target blocks active; the others have between (66) // 3 and 32. `block_index`: within each batch group, the 512 entries of its rows name each of the group's source blocks exactly once.
All inputs are finite; a program needn't handle non-finite values.
Results may differ from a plain program's by a relative error of at most 0.0045.
Values may be sent and summed in bfloat16 or wider, within the bound.
A program may use at most 128 MiB of HBM per device.

v0:
```python
import jax
import jax.numpy as jnp
from jax import lax
from jax.sharding import PartitionSpec as P

BLOCK = 64


def aggregate_rows(values, index, weights):
    width_here = values.shape[1]
    tiled = values.reshape(-1, BLOCK, width_here)
    chosen = jnp.take(tiled, index, axis=0)
    chosen = chosen.reshape(index.shape[0], -1, width_here)
    summed = jnp.einsum("tim,tmc->tic", weights, chosen, preferred_element_type=jnp.float32)
    totals = jnp.sum(weights.astype(jnp.float32), axis=2)
    return (summed / totals[..., None]).astype(jnp.bfloat16).reshape(-1, width_here)


def body(
    feature_store,
    requests,
    block_index,
    block_values,
    frontier,
    self_first,
    neigh_first,
    bias_first,
    second_index,
    second_values,
    self_second,
    neigh_second,
    bias_second,
    classifier,
    bias_class,
):
    feat_count = lax.axis_size("feat")
    feat_place = lax.axis_index("feat")
    width_here = feature_store.shape[0]
    store_rows = jnp.transpose(feature_store)
    picked = jnp.take(
        store_rows,
        lax.all_to_all(requests, "batch", split_axis=0, concat_axis=0, tiled=True),
        axis=0,
    )
    fetched = lax.all_to_all(picked, "batch", split_axis=0, concat_axis=0, tiled=True)
    sources = fetched.reshape(-1, width_here)
    block_count = block_index.shape[0]
    target_rows = block_count * BLOCK
    own_rows = target_rows // feat_count
    own_blocks = block_count // feat_count
    full_sources = lax.all_gather(sources, "feat", axis=1, tiled=True)
    own_index = lax.dynamic_slice_in_dim(block_index, feat_place * own_blocks, own_blocks, 0)
    own_values = lax.dynamic_slice_in_dim(block_values, feat_place * own_blocks, own_blocks, 0)
    aggregated = aggregate_rows(full_sources, own_index, own_values)
    own_self = lax.dynamic_slice_in_dim(full_sources, feat_place * own_rows, own_rows, 0)
    pre_first = jnp.dot(own_self, self_first, preferred_element_type=jnp.float32) + jnp.dot(
        aggregated, neigh_first, preferred_element_type=jnp.float32
    )
    block_number = feat_place * own_blocks + jnp.arange(own_rows, dtype=jnp.int32) // BLOCK
    active = block_number < frontier[0]
    layer_one = jnp.where(active[:, None], jnp.maximum(pre_first + bias_first, 0.0), 0.0).astype(
        jnp.bfloat16
    )
    every_row = lax.all_gather(layer_one, "feat", axis=0, tiled=True)
    hidden_width = every_row.shape[1]
    tiles = every_row.reshape(block_count, BLOCK, hidden_width)
    chosen_two = jnp.take(tiles, second_index, axis=0).reshape(
        second_index.shape[0], -1, hidden_width
    )
    summed_two = jnp.einsum(
        "tim,tmh->tih", second_values, chosen_two, preferred_element_type=jnp.float32
    )
    totals_two = jnp.sum(second_values.astype(jnp.float32), axis=2)
    aggregated_two = (summed_two / totals_two[..., None]).astype(jnp.bfloat16).reshape(own_rows, -1)
    pre_second = (
        jnp.dot(layer_one, self_second, preferred_element_type=jnp.float32)
        + jnp.dot(aggregated_two, neigh_second, preferred_element_type=jnp.float32)
        + bias_second
    )
    layer_two = jnp.where(active[:, None], jnp.maximum(pre_second, 0.0), 0.0).astype(jnp.bfloat16)
    return jnp.dot(layer_two, classifier, preferred_element_type=jnp.float32) + bias_class


def solution(mesh):
    in_specs = (
        P("feat", "batch"),
        P("batch", None),
        P("batch", None),
        P("batch", None, None),
        P("batch"),
        P(),
        P(),
        P(),
        P(("batch", "feat"), None),
        P(("batch", "feat"), None, None),
        P(),
        P(),
        P(),
        P(),
        P(),
    )
    out_specs = P(("batch", "feat"), None)
    return jax.shard_map(body, mesh=mesh, in_specs=in_specs, out_specs=out_specs, check_vma=False)
```

profile of v0, /device:TPU:1, one launch (start us, length us, event | category | flops | bytes accessed | tf_op | source)
XLA Modules:
  0.0 303.1 jit_solution(1855548085714292098)
XLA Ops:
  6.5 1.7 all_to_all.13
  8.2 12.0 %all-to-all-start = ((s32[64,1,512]{2,1,0:T(1,128)}), s32[64,1,512]{2,1,0:T(1,128)S(1)}, u32[]{:S(2)}, u32[]{:S(2)}) async-start(s32[64,1,512]{2,1,0:T(1,128)} %all_to_all.13), calls=%async_computation | async-start | bytes 262144 | tf_op jit(solution)/shard_map/all_to_all | solution.py:42
  20.2 4.9 %copy.31 = bf16[64,16384]{0,1:T(8,128)(2,1)} copy(bf16[64,16384]{1,0:T(8,128)(2,1)} %param.15) | data formatting | bytes 4194304 | tf_op args[0]
  25.1 3.8 %all-to-all-done = s32[64,1,512]{2,1,0:T(1,128)S(1)} async-done(((s32[64,1,512]{2,1,0:T(1,128)}), s32[64,1,512]{2,1,0:T(1,128)S(1)}, u32[]{:S(2)}, u32[]{:S(2)}) %all-to-all-start) | async-done | bytes 131104 | tf_op jit(solution)/shard_map/all_to_all | solution.py:42
  29.0 0.1 compare_select_fusion
  29.1 112.9 %gather_fusion = bf16[32768,64]{1,0:T(8,128)(2,1)} fusion(bf16[16384,64]{1,0:T(8,128)(2,1)} %bitcast.36, s32[32768]{0:T(1024)S(1)} %broadcast_clamp_fusion), kind=kCustom, calls=%fused_computation | custom fusion | bytes 8519680 | tf_op jit(solution)/shard_map/jit(_take)/gather | solution.py:40
  142.1 8.5 %copy.32 = bf16[64,512,64]{1,2,0:T(8,128)(2,1)} copy(bf16[64,512,64]{2,1,0:T(8,128)(2,1)} %bitcast.38) | data formatting | bytes 8388608 | tf_op jit(solution)/shard_map/jit(_take)/gather | solution.py:40
  150.7 2.6 broadcast_select_fusion
  153.3 56.3 %all_to_all.20 = bf16[64,512,64]{1,2,0:T(8,128)(2,1)S(1)} all-to-all(bf16[64,512,64]{1,2,0:T(8,128)(2,1)S(1)} %broadcast_select_fusion), channel_id=1, replica_groups=mesh['batch'=64,'feat'=2] {'batch'}, dimensions={0} | all-to-all | bytes 8388608 | tf_op jit(solution)/shard_map/all_to_all | solution.py:45
  209.6 2.3 copy.40
  212.0 0.2 all-gather.5.cloned.1.call-start
  212.2 0.4 copy-done.9
  212.7 0.1 copy.34
  212.8 0.1 broadcast_in_dim.66
  212.9 0.1 broadcast_in_dim.67
  213.8 1.9 convert_reduce_fusion.1
  215.8 18.1 %all-gather.3.cloned.1.call-done = bf16[32768,128]{0,1:T(8,128)(2,1)} async-done(((bf16[32768,64]{0,1:T(8,128)(2,1)}), bf16[32768,128]{0,1:T(8,128)(2,1)}) %all-gather.3.cloned.1.call-update) | async-done | bytes 8388624 | tf_op jit(solution)/shard_map/all_gather | solution.py:51
  233.9 11.4 %copy.35 = bf16[32768,128]{1,0:T(8,128)(2,1)} copy(bf16[32768,128]{0,1:T(8,128)(2,1)} %all-gather.3.cloned.1.call-done) | data formatting | bytes 16777216 | tf_op jit(solution)/shard_map/all_gather | solution.py:51
  245.3 6.4 %gather_fusion.1 = bf16[256,64,128]{2,1,0:T(8,128)(2,1)} fusion(bf16[512,64,128]{2,1,0:T(8,128)(2,1)} %bitcast.40, s32[1024]{0:T(1024)S(1)} %pad_clamp_fusion.1), kind=kCustom, calls=%fused_computation.1 | custom fusion | bytes 8389632 | tf_op jit(solution)/shard_map/jit(_take)/gather | solution.py:12
  251.8 6.2 %bitcast_select_fusion.1 = bf16[32,512,128]{2,1,0:T(8,128)(2,1)S(1)} fusion(pred[32,512]{1,0:T(8,128)(4,1)S(1)} %broadcast_in_dim.67, bf16[32,512,128]{2,1,0:T(8,128)(2,1)} %bitcast.42), kind=kLoop, calls=%fused_computation.4 | loop fusion | flops 2097152 | bytes 8404992 | tf_op jit(solution)/shard_map/jit(_take)/select_n | solution.py:12
  258.0 0.9 fusion.13
  259.0 1.7 fusion.19
  260.7 1.5 fusion.6
  262.3 0.1 broadcast_in_dim.71
  262.4 0.1 broadcast_in_dim.72
  262.7 0.3 convert_reduce_fusion
  263.1 1.7 fusion.29
  264.8 12.2 %all-gather.5.cloned.1.call-done = bf16[4096,256]{1,0:T(8,128)(2,1)} async-done(((bf16[2048,256]{1,0:T(8,128)(2,1)}), bf16[4096,256]{1,0:T(8,128)(2,1)}) %all-gather.5.cloned.1.call-update) | async-done | bytes 2097168 | tf_op jit(solution)/shard_map/all_gather | solution.py:64
  277.0 10.2 %gather_fusion.2 = bf16[256,64,256]{2,1,0:T(8,128)(2,1)} fusion(bf16[64,64,256]{2,1,0:T(8,128)(2,1)} %bitcast.39, s32[1024]{0:T(1024)S(1)} %pad_clamp_fusion), kind=kCustom, calls=%fused_computation.2 | custom fusion | bytes 16778240 | tf_op jit(solution)/shard_map/jit(_take)/gather | solution.py:67
  287.2 5.5 %bitcast_select_fusion = bf16[32,512,256]{2,1,0:T(8,128)(2,1)S(1)} fusion(pred[32,512]{1,0:T(8,128)(4,1)S(1)} %broadcast_in_dim.72, bf16[32,512,256]{2,1,0:T(8,128)(2,1)} %bitcast.37), kind=kLoop, calls=%fused_computation.3 | loop fusion | flops 4194304 | bytes 16793600 | tf_op jit(solution)/shard_map/jit(_take)/select_n | solution.py:67
  292.7 1.5 divide_convert_fusion
  294.3 2.0 convolution_add_fusion.2
  (41 shorter events, 0.7 us)
Async XLA Ops:
  6.5 256.6 %copy-start = (bf16[256,256]{1,0:T(8,128)(2,1)S(1)}, bf16[256,256]{1,0:T(8,128)(2,1)}, u32[]{:S(2)}) copy-start(bf16[256,256]{1,0:T(8,128)(2,1)} %param.25) | copy-start | bytes 393220
  8.2 20.7 %all-to-all-start = ((s32[64,1,512]{2,1,0:T(1,128)}), s32[64,1,512]{2,1,0:T(1,128)S(1)}, u32[]{:S(2)}, u32[]{:S(2)}) async-start(s32[64,1,512]{2,1,0:T(1,128)} %all_to_all.13), calls=%async_computation | async-start | bytes 262144 | tf_op jit(solution)/shard_map/all_to_all | solution.py:42
  20.2 213.7 %all-gather.3.cloned.1.call-start = ((), (), s32[]{:S(2)}) async-start(), calls=%async_computation.2 | async-start | bytes 12582912 | tf_op jit(solution)/shard_map/all_gather | solution.py:51
  211.9 0.7 copy-start.9
  212.0 65.0 %all-gather.5.cloned.1.call-start = ((), (), s32[]{:S(2)}) async-start(), calls=%async_computation.3 | async-start | bytes 3145728 | tf_op jit(solution)/shard_map/all_gather | solution.py:64
  251.8 6.2 %copy-start.3 = (bf16[64,64,512]{2,1,0:T(8,128)(2,1)S(1)}, bf16[64,64,512]{2,1,0:T(8,128)(2,1)}, u32[]{:S(2)}) copy-start(bf16[64,64,512]{2,1,0:T(8,128)(2,1)} %param.18) | copy-start | bytes 12582916
  258.0 1.0 copy-start.7
  258.0 2.7 copy-start.6
  258.0 2.6 copy-start.10
  259.0 3.2 %copy-start.8 = (s32[32,8]{0,1:T(8,128)S(1)}, s32[32,8]{0,1:T(8,128)}, u32[]{:S(2)}) copy-start(s32[32,8]{0,1:T(8,128)} %param.23) | copy-start | bytes 3076
  259.0 3.7 %copy-start.1 = (bf16[32,64,512]{2,1,0:T(8,128)(2,1)S(1)}, bf16[32,64,512]{2,1,0:T(8,128)(2,1)}, u32[]{:S(2)}) copy-start(bf16[32,64,512]{2,1,0:T(8,128)(2,1)} %param.24) | copy-start | bytes 6291460
  287.2 5.5 %copy-start.2 = (bf16[32,64,512]{2,1,0:T(8,128)(2,1)S(1)}, bf16[32,64,512]{2,1,0:T(8,128)(2,1)}, u32[]{:S(2)}) copy-start(bf16[32,64,512]{2,1,0:T(8,128)(2,1)} %param.24) | copy-start | bytes 6291460
  292.7 1.6 copy-start.4
  292.7 1.6 copy-start.5
  292.7 1.6 copy-start.11
  292.7 1.5 copy-start.12
Sparse Core Ops, SparseCore 0:
  212.1 21.8 all-gather.2
  262.3 14.6 all-gather.4
where the time goes:
time: 304 us; the launch traced here: 303 us
  local copies, waits for them, and re-layouts  160 us (53%)
  blocking collectives  56.3 us (19%)
  waiting for transfers between devices  34.2 us (11%)
  other arithmetic  16.9 us (6%)
  between operations  14.4 us (5%)
  starting transfers between devices  12.2 us (4%)
  matrix products  9.2 us (3%)
    gather x2, local copies, waits for them, and re-layouts, body(): jnp.take(store_rows, lax.all_to_all(requests, 'batch', split_axis=0, conc...  121 us
    all_to_all x1, blocking collectives, body(): lax.all_to_all(picked, 'batch', split_axis=0, concat_axis=0, tiled=True)  56.3 us
    all_gather x1, waiting for transfers between devices, body(): full_sources = lax.all_gather(sources, 'feat', axis=1, tiled=True)  18.1 us
    all_gather x1, waiting for transfers between devices, body(): every_row = lax.all_gather(layer_one, 'feat', axis=0, tiled=True)  12.2 us
    all_to_all x1, starting transfers between devices, body(): lax.all_to_all(requests, 'batch', split_axis=0, concat_axis=0, tiled=True)  12 us
    all_gather x1, local copies, waits for them, and re-layouts, body(): full_sources = lax.all_gather(sources, 'feat', axis=1, tiled=True)  11.4 us
    gather x1, local copies, waits for them, and re-layouts, body(): jnp.take(tiles, second_index, axis=0)  10.2 us
    gather x1, local copies, waits for them, and re-layouts, aggregate_rows(): chosen = jnp.take(tiled, index, axis=0)  6.43 us
  transfers between devices with their start and end apart: 3, of which 3 were waited for; matrix products, arithmetic and copies ran while one was open for 3% of the time, Pallas kernels for 0%

commit v1 on v0

v1 whole, which is shorter than its diff:
```python
import functools

import jax
import jax.numpy as jnp
from jax import lax
from jax.experimental import pallas as pl
from jax.experimental.pallas import tpu as pltpu
from jax.sharding import PartitionSpec as P

MESH = pl.DeviceIdType.MESH
BLOCK = 64
GROUPS = 64
HALF_CAP = 256
FEAT = 128
HID = 256
TB = 64
OWN_TB = 32
NBR = 8
STORE = 16384
CHUNKS = 4
ROW_CHUNKS = 8


def torus_order():
    def orbit(t):
        z, y, x = t
        found = []
        for r in ((z, y, x), (y, x, z), (x, z, y)):
            for n in (r, tuple((-v) % 4 for v in r)):
                if n not in found:
                    found.append(n)
        return found

    seen, orbits = set(), []
    for s in range(1, GROUPS):
        t = (s // 16, (s // 4) % 4, s % 4)
        if t not in seen:
            o = orbit(t)
            seen.update(o)
            orbits.append(o)
    left = sorted(orbits, key=lambda o: -sum(min(d, 4 - d) for d in o[0]))
    mixed = []
    while left:
        mixed.append(left.pop(0))
        if left:
            mixed.append(left.pop())
    return [t[0] * 16 + t[1] * 4 + t[2] for o in mixed for t in o]


ORDER = torus_order()
WORDS = [
    sum(s * 64**e for e, s in enumerate(ORDER[w : w + 5])) for w in range(0, GROUPS - 1, 5)
]


def shift_of(i):
    word = jnp.int32(WORDS[0])
    for w in range(1, len(WORDS)):
        word = jnp.where(i // 5 == w, jnp.int32(WORDS[w]), word)
    place = lax.rem(i, 5)
    shift = lax.rem(word, 64)
    for e in range(1, 5):
        shift = jnp.where(place == e, lax.rem(word // 64**e, 64), shift)
    return shift


def peer(me, s):
    z, y, x = me // 16, (me // 4) % 4, me % 4
    dz, dy, dx = s // 16, (s // 4) % 4, s % 4
    return ((z + dz) % 4) * 16 + ((y + dy) % 4) * 4 + (x + dx) % 4


def first_kernel(
    store_hbm,
    req,
    places,
    mine,
    values_hbm,
    frontier,
    w_self,
    w_neigh,
    bias,
    out,
    cols,
    rows,
    sreq,
    rreq,
    idx,
    tmp,
    sendbuf,
    rbuf,
    values,
    psend,
    precv,
    totals,
    selfbuf,
    agg,
    chosen,
    l1,
    load_sem,
    half_send,
    half_recv,
    req_send,
    req_recv,
    idx_sem,
    msg_send,
    msg_recv,
    p_send,
    p_recv,
    self_send,
    self_recv,
    self_own,
    l1_send,
    l1_recv,
    l1_own,
):
    me = lax.axis_index("batch")
    c = lax.axis_index("feat")
    sib = 1 - c

    barrier = pltpu.get_barrier_semaphore()
    pl.semaphore_signal(barrier, inc=1, device_id=(me, sib), device_id_type=MESH)

    def greet(s, _):
        pl.semaphore_signal(
            barrier, inc=1, device_id=(lax.rem(me + s, GROUPS), c), device_id_type=MESH
        )
        return 0

    lax.fori_loop(1, GROUPS, greet, 0)

    width = STORE // CHUNKS
    half = pl.ds(pl.multiple_of(c * 64, 64), 64)
    own_load = pltpu.make_async_copy(store_hbm, cols.at[half], load_sem.at[0])
    own_load.start()
    values_load = pltpu.make_async_copy(values_hbm, values, load_sem.at[1])
    values_load.start()
    for h in range(2):
        sreq[:, h, :] = req[:, pl.ds(pl.multiple_of(c * HALF_CAP + h * 128, 128), 128)]
    rreq[me] = sreq[me]
    pl.semaphore_wait(barrier, GROUPS)

    def req_copy(s):
        p = lax.rem(me + s, GROUPS)
        return pltpu.make_async_remote_copy(
            src_ref=sreq.at[p],
            dst_ref=rreq.at[me],
            send_sem=req_send.at[s],
            recv_sem=req_recv.at[s],
            device_id=(p, c),
            device_id_type=MESH,
        )

    def req_start(s, _):
        req_copy(s).start()
        return 0

    lax.fori_loop(1, GROUPS, req_start, 0)

    def half_copy(j):
        part = pl.ds(j * width, width)
        return pltpu.make_async_remote_copy(
            src_ref=store_hbm.at[:, part],
            dst_ref=cols.at[half, part],
            send_sem=half_send.at[j],
            recv_sem=half_recv.at[j],
            device_id=(me, sib),
            device_id_type=MESH,
        )

    for j in range(CHUNKS):
        half_copy(j).start()
    own_load.wait()
    for j in range(CHUNKS):
        half_copy(j).wait_recv()

        def turn(i, _):
            at = pl.multiple_of(j * width + i * 512, 512)
            rows[pl.ds(at, 512), :] = cols[:, pl.ds(at, 512)].T.astype(jnp.float32)
            return 0

        lax.fori_loop(0, width // 512, turn, 0)

    def req_wait(s, _):
        req_copy(s).wait_recv()
        return 0

    lax.fori_loop(1, GROUPS, req_wait, 0)
    idx_copy = pltpu.make_async_copy(rreq, idx, idx_sem)
    idx_copy.start()
    idx_copy.wait()

    def gather(p):
        for h in range(2):
            for q in range(128):
                tmp[pl.ds(h * 128 + q, 1), :] = rows[pl.ds(idx[p, h, q], 1), :]
        return tmp[...].astype(jnp.bfloat16).reshape(4, BLOCK, FEAT)

    def msg_copy(s):
        p = peer(me, s)
        return pltpu.make_async_remote_copy(
            src_ref=sendbuf.at[pl.ds(p * 4, 4)],
            dst_ref=rbuf.at[pl.ds(me * 4, 4)],
            send_sem=msg_send.at[s],
            recv_sem=msg_recv.at[s],
            device_id=(p, c),
            device_id_type=MESH,
        )

    def msg_start(i, _):
        s = shift_of(i)
        p = peer(me, s)
        sendbuf[pl.ds(p * 4, 4)] = gather(p)
        msg_copy(s).start()
        return 0

    lax.fori_loop(0, GROUPS - 1, msg_start, 0)
    rbuf[pl.ds(me * 4, 4)] = gather(me)

    values_load.wait()
    ones = jnp.ones((512, FEAT), jnp.bfloat16)

    def total(t, _):
        totals[t] = jnp.dot(values[c * OWN_TB + t], ones, preferred_element_type=jnp.float32)
        return 0

    lax.fori_loop(0, OWN_TB, total, 0)

    def msg_wait(s, _):
        msg_copy(s).wait_recv()
        return 0

    lax.fori_loop(1, GROUPS, msg_wait, 0)

    def self_copy(j):
        return pltpu.make_async_remote_copy(
            src_ref=rbuf.at[pl.ds((sib * 4 + j) * 4, 4)],
            dst_ref=selfbuf.at[2 * j + c],
            send_sem=self_send.at[j],
            recv_sem=self_recv.at[j],
            device_id=(me, sib),
            device_id_type=MESH,
        )

    def self_local(j):
        return pltpu.make_async_copy(
            rbuf.at[pl.ds((c * 4 + j) * 4, 4)], selfbuf.at[2 * j + c], self_own.at[j]
        )

    for j in range(4):
        self_copy(j).start()
        self_local(j).start()

    def partial_sum(t, slot):
        for k in range(NBR):
            chosen[slot, pl.ds(k * BLOCK, BLOCK), :] = rbuf[places[t, k]]
        weights = values[t] * mine[pl.ds(t, 1), :].astype(jnp.bfloat16)
        return jnp.dot(weights, chosen[slot], preferred_element_type=jnp.float32)

    def p_copy(m):
        return pltpu.make_async_remote_copy(
            src_ref=psend.at[pl.ds(m * 8, 8)],
            dst_ref=precv.at[pl.ds(m * 8, 8)],
            send_sem=p_send.at[m],
            recv_sem=p_recv.at[m],
            device_id=(me, sib),
            device_id_type=MESH,
        )

    for m in range(4):

        def other(i, _):
            for u in range(4):
                t = m * 8 + i * 4 + u
                psend[t] = partial_sum(sib * OWN_TB + t, u)
            return 0

        lax.fori_loop(0, 2, other, 0)
        p_copy(m).start()

    def own(i, _):
        for u in range(4):
            t = i * 4 + u
            agg[t] = partial_sum(c * OWN_TB + t, u)
        return 0

    lax.fori_loop(0, OWN_TB // 4, own, 0)

    def l1_copy(m):
        at = pl.multiple_of(c * 2048 + m * 256, 256)
        return pltpu.make_async_remote_copy(
            src_ref=l1.at[pl.ds(m * 256, 256)],
            dst_ref=out.at[pl.ds(at, 256)],
            send_sem=l1_send.at[m],
            recv_sem=l1_recv.at[m],
            device_id=(me, sib),
            device_id_type=MESH,
        )

    def l1_local(m):
        at = pl.multiple_of(c * 2048 + m * 256, 256)
        return pltpu.make_async_copy(
            l1.at[pl.ds(m * 256, 256)], out.at[pl.ds(at, 256)], l1_own.at[m]
        )

    for j in range(4):
        self_copy(j).wait_recv()
        self_local(j).wait()
    for m in range(ROW_CHUNKS):
        if m % 2 == 0:
            p_copy(m // 2).wait_recv()
        mean = (agg[pl.ds(m * 4, 4)] + precv[pl.ds(m * 4, 4)]) / totals[pl.ds(m * 4, 4)]
        mean = mean.astype(jnp.bfloat16).reshape(256, FEAT)
        pre = (
            jnp.dot(selfbuf[m].reshape(256, FEAT), w_self[...], preferred_element_type=jnp.float32)
            + jnp.dot(mean, w_neigh[...], preferred_element_type=jnp.float32)
            + bias[...]
        )
        number = c * OWN_TB + m * 4 + lax.broadcasted_iota(jnp.int32, (256, HID), 0) // BLOCK
        layer = jnp.where(number < frontier[0], jnp.maximum(pre, 0.0), 0.0)
        l1[pl.ds(m * 256, 256), :] = layer.astype(jnp.bfloat16)
        l1_copy(m).start()
        l1_local(m).start()

    for m in range(ROW_CHUNKS):
        l1_copy(m).wait()
        l1_local(m).wait()
    for j in range(CHUNKS):
        half_copy(j).wait_send()
    for j in range(4):
        self_copy(j).wait_send()
        p_copy(j).wait_send()

    def sent(s, _):
        req_copy(s).wait_send()
        msg_copy(s).wait_send()
        return 0

    lax.fori_loop(1, GROUPS, sent, 0)


def second_kernel(
    rows, second_index, frontier, values, w_self, w_neigh, bias, w_class, bias_class, out, chosen
):
    m = pl.program_id(0)
    c = lax.axis_index("feat")
    ones = jnp.ones((512, 128), jnp.bfloat16)
    means = []
    for u in range(4):
        for k in range(NBR):
            at = pl.multiple_of(second_index[m * 4 + u, k] * BLOCK, BLOCK)
            chosen[u, pl.ds(k * BLOCK, BLOCK), :] = rows[pl.ds(at, BLOCK), :]
        summed = jnp.dot(values[u], chosen[u], preferred_element_type=jnp.float32)
        total = jnp.dot(values[u], ones, preferred_element_type=jnp.float32)
        total = jnp.concatenate([total, total], axis=1)
        means.append((summed / total).astype(jnp.bfloat16))
    mean = jnp.concatenate(means, axis=0)
    own = rows[pl.ds(pl.multiple_of(c * 2048 + m * 256, 256), 256), :]
    pre = (
        jnp.dot(own, w_self[...], preferred_element_type=jnp.float32)
        + jnp.dot(mean, w_neigh[...], preferred_element_type=jnp.float32)
        + bias[...]
    )
    number = c * OWN_TB + m * 4 + lax.broadcasted_iota(jnp.int32, (256, HID), 0) // BLOCK
    layer = jnp.where(number < frontier[0], jnp.maximum(pre, 0.0), 0.0).astype(jnp.bfloat16)
    out[...] = (
        lax.dot_general(
            w_class[...], layer, (((1,), (1,)), ((), ())), preferred_element_type=jnp.float32
        )
        + bias_class[...]
    )


def body(
    feature_store,
    requests,
    block_index,
    block_values,
    frontier,
    self_first,
    neigh_first,
    bias_first,
    second_index,
    second_values,
    self_second,
    neigh_second,
    bias_second,
    classifier,
    bias_class,
):
    vmem = pl.BlockSpec(memory_space=pltpu.VMEM)
    smem = pl.BlockSpec(memory_space=pltpu.SMEM)
    hbm = pl.BlockSpec(memory_space=pl.ANY)
    dma = pltpu.SemaphoreType.DMA
    bf16, f32, i32 = jnp.bfloat16, jnp.float32, jnp.int32
    places = block_index // 8 * 4 + block_index % 4
    held = (block_index // 4 % 2 == lax.axis_index("feat")).astype(f32)
    mine = jnp.repeat(held, BLOCK, axis=1)
    layer_one = pl.pallas_call(
        first_kernel,
        out_shape=jax.ShapeDtypeStruct((TB * BLOCK, HID), bf16),
        in_specs=[hbm, vmem, smem, vmem, hbm, smem, vmem, vmem, vmem],
        out_specs=hbm,
        scratch_shapes=[
            pltpu.VMEM((FEAT, STORE), bf16),
            pltpu.VMEM((STORE, FEAT), f32),
            pltpu.VMEM((GROUPS, 2, 128), i32),
            pltpu.VMEM((GROUPS, 2, 128), i32),
            pltpu.SMEM((GROUPS, 2, 128), i32),
            pltpu.VMEM((HALF_CAP, FEAT), f32),
            pltpu.VMEM((GROUPS * 4, BLOCK, FEAT), bf16),
            pltpu.VMEM((GROUPS * 4, BLOCK, FEAT), bf16),
            pltpu.VMEM((TB, BLOCK, NBR * BLOCK), bf16),
            pltpu.VMEM((OWN_TB, BLOCK, FEAT), f32),
            pltpu.VMEM((OWN_TB, BLOCK, FEAT), f32),
            pltpu.VMEM((OWN_TB, BLOCK, FEAT), f32),
            pltpu.VMEM((8, 4, BLOCK, FEAT), bf16),
            pltpu.VMEM((OWN_TB, BLOCK, FEAT), f32),
            pltpu.VMEM((4, NBR * BLOCK, FEAT), bf16),
            pltpu.VMEM((OWN_TB * BLOCK, HID), bf16),
            dma((2,)),
            dma((CHUNKS,)),
            dma((CHUNKS,)),
            dma((GROUPS,)),
            dma((GROUPS,)),
            dma,
            dma((GROUPS,)),
            dma((GROUPS,)),
            dma((4,)),
            dma((4,)),
            dma((4,)),
            dma((4,)),
            dma((4,)),
            dma((ROW_CHUNKS,)),
            dma((ROW_CHUNKS,)),
            dma((ROW_CHUNKS,)),
        ],
        compiler_params=pltpu.CompilerParams(
            collective_id=0, has_side_effects=True, vmem_limit_bytes=48 * 2**20
        ),
        name="layer_one",
    )(
        feature_store,
        requests,
        places,
        mine,
        block_values,
        frontier,
        self_first,
        neigh_first,
        bias_first.reshape(1, HID),
    )
    classes = classifier.shape[1]
    whole = lambda *shape: pl.BlockSpec(shape, lambda m: (0,) * len(shape))
    logits = pl.pallas_call(
        second_kernel,
        grid=(ROW_CHUNKS,),
        out_shape=jax.ShapeDtypeStruct((classes, OWN_TB * BLOCK), f32),
        in_specs=[
            whole(TB * BLOCK, HID),
            smem,
            smem,
            pl.BlockSpec((4, BLOCK, NBR * BLOCK), lambda m: (m, 0, 0)),
            whole(HID, HID),
            whole(HID, HID),
            whole(1, HID),
            whole(classes, HID),
            whole(classes, 1),
        ],
        out_specs=pl.BlockSpec((classes, 256), lambda m: (0, m)),
        scratch_shapes=[pltpu.VMEM((4, NBR * BLOCK, HID), bf16)],
        compiler_params=pltpu.CompilerParams(vmem_limit_bytes=32 * 2**20),
        name="layer_two",
    )(
        layer_one,
        second_index,
        frontier,
        second_values,
        self_second,
        neigh_second,
        bias_second.reshape(1, HID),
        classifier.T,
        bias_class.reshape(classes, 1),
    )
    return logits.T


def solution(mesh):
    in_specs = (
        P("feat", "batch"),
        P("batch", None),
        P("batch", None),
        P("batch", None, None),
        P("batch"),
        P(),
        P(),
        P(),
        P(("batch", "feat"), None),
        P(("batch", "feat"), None, None),
        P(),
        P(),
        P(),
        P(),
        P(),
    )
    out_specs = P(("batch", "feat"), None)
    return jax.shard_map(body, mesh=mesh, in_specs=in_specs, out_specs=out_specs, check_vma=False)
```

time: 304 us -> 104 us (0.34)
  local copies, waits for them, and re-layouts: 160 us -> 7.43 us
  Pallas kernels: 0 us -> 94.9 us
  blocking collectives: 56.3 us -> 0 us
  waiting for transfers between devices: 34.2 us -> 0 us
  other arithmetic: 16.9 us -> 0.07 us
  between operations: 14.4 us -> 0.75 us
  starting transfers between devices: 12.2 us -> 0 us
  matrix products: 9.2 us -> 0 us
    gather x4 -> x0, local copies, waits for them, and re-layouts: 138 us -> none  [the longest x2 121 us: body(): jnp.take(store_rows, lax.all_to_all(requests, 'batch', split_axis=0, conc...]
    pallas_call x0 -> x2, Pallas kernels: none -> 94.9 us  [the longest x1 86.9 us: body(): pl.pallas_call(first_kernel, out_shape=jax.ShapeDtypeStruct((TB * BLOCK,...]
    all_to_all x1 -> x0, blocking collectives: 56.3 us -> none  [body(): lax.all_to_all(picked, 'batch', split_axis=0, concat_axis=0, tiled=True)]
    all_gather x2 -> x0, waiting for transfers between devices: 30.3 us -> none  [the longest x1 18.1 us: body(): full_sources = lax.all_gather(sources, 'feat', axis=1, tiled=True)]
    select_n x5 -> x0, other arithmetic: 14.4 us -> none  [the longest x1 6.22 us: aggregate_rows(): chosen = jnp.take(tiled, index, axis=0)]
    all_to_all x1 -> x0, starting transfers between devices: 12 us -> none  [body(): lax.all_to_all(requests, 'batch', split_axis=0, concat_axis=0, tiled=True)]
    all_gather x1 -> x0, local copies, waits for them, and re-layouts: 11.4 us -> none  [body(): full_sources = lax.all_gather(sources, 'feat', axis=1, tiled=True)]
    dot_general x6 -> x0, matrix products: 9.2 us -> none  [the longest x1 1.99 us: body(): jnp.dot(layer_two, classifier, preferred_element_type=jnp.float32)]
  transfers between devices with their start and end apart: 3 -> 0, of which waited for: 3 -> 0; matrix products, arithmetic and copies ran while one was open for 3% -> 0% of each run, Pallas kernels for 0% -> 0%
where the time goes in v1:
time: 104 us; the launch traced here: 103 us
  Pallas kernels  94.9 us (91%)
  local copies, waits for them, and re-layouts  7.43 us (7%)
    pallas_call x1, Pallas kernels, body(): pl.pallas_call(first_kernel, out_shape=jax.ShapeDtypeStruct((TB * BLOCK,...  86.9 us
    pallas_call x1, Pallas kernels, body(): pl.pallas_call(second_kernel, grid=(ROW_CHUNKS,), out_shape=jax.ShapeDtyp...  8.02 us
    unnamed x22, local copies, waits for them, and re-layouts  6.4 us

profile of v1, /device:TPU:1, one launch (start us, length us, event | category | flops | bytes accessed | tf_op | source)
XLA Modules:
  0.0 103.2 jit_solution(13210902414119480415)
XLA Ops:
  0.7 0.8 copy.25.second_index
  1.4 0.8 copy.21
  2.3 0.8 copy.26.bias_class
  3.1 0.1 broadcast_in_dim.3
  3.2 0.1 reshape.12.mine
  3.3 0.0 copy-start
  3.3 1.6 %copy-done = bf16[64,16384]{1,0:T(8,128)(2,1)S(1)} copy-done((bf16[64,16384]{1,0:T(8,128)(2,1)S(1)}, bf16[64,16384]{1,0:T(8,128)(2,1)}, u32[]{:S(2)}) %copy-start) | copy-done | bytes 2097176
  4.9 0.0 copy-start.2
  4.9 0.9 copy-done.2
  5.8 0.0 copy-start.6
  5.8 0.8 copy-done.6
  6.7 0.0 copy-start.7
  6.7 0.8 copy-done.7
  7.5 0.0 copy-start.8
  7.5 0.7 copy-done.8
  8.2 0.0 copy-start.1
  8.2 0.0 copy-start.3
  8.2 0.0 copy-start.4
  8.2 0.0 copy-start.5
  8.2 0.0 copy-start.9
  8.2 86.9 %layer_one.1.rows = bf16[4096,256]{1,0:T(8,128)(2,1)S(1)} custom-call(bf16[64,16384]{1,0:T(8,128)(2,1)S(1)} %copy-done, s32[64,512]{1,0:T(8,128)S(1)} %copy-done.2, s32[64,8]{1,0:T(8,128)S(1)} %fusion.2.places, f32[64,512]{1,0:T(8,128)S(1)} %reshape.12.mine, bf16[64,64,512]{2,1,0:T(8,128)(2,1)} %values_hbm.1, s32[1]{0:T(128)S(6)} %copy.27.frontier, ...), custom_call_target="tpu_custom_call" | custom-call | tf_op jit(solution)/shard_map/layer_one/pallas_call | solution.py:399
  95.1 0.0 copy-done.1
  95.1 0.0 copy-done.3
  95.1 0.0 copy-done.4
  95.1 0.0 copy-done.5
  95.2 0.0 copy-done.9
  95.2 8.0 %layer_two.1 = f32[172,2048]{1,0:T(8,128)} custom-call(bf16[4096,256]{1,0:T(8,128)(2,1)S(1)} %layer_one.1.rows, s32[32,8]{1,0:T(8,128)S(1)} %copy.25.second_index, s32[1]{0:T(128)S(6)} %copy.27.frontier, bf16[32,64,512]{2,1,0:T(8,128)(2,1)S(1)} %copy-done.1, bf16[256,256]{1,0:T(8,128)(2,1)S(1)} %copy-done.3, bf16[256,256]{1,0:T(8,128)(2,1)S(1)} %copy-done.4, ...), custom_call_target="tpu_custom_call" | custom-call | tf_op jit(solution)/shard_map/layer_two/pallas_call | solution.py:455
  (2 shorter events, 0.1 us)
Async XLA Ops:
  3.3 1.6 %copy-start = (bf16[64,16384]{1,0:T(8,128)(2,1)S(1)}, bf16[64,16384]{1,0:T(8,128)(2,1)}, u32[]{:S(2)}) copy-start(bf16[64,16384]{1,0:T(8,128)(2,1)} %store_hbm.1) | copy-start | bytes 6291460
  4.9 0.9 copy-start.2
  5.8 0.8 copy-start.6
  6.7 0.8 copy-start.7
  7.5 0.7 copy-start.8
  8.2 86.9 %copy-start.1 = (bf16[32,64,512]{2,1,0:T(8,128)(2,1)S(1)}, bf16[32,64,512]{2,1,0:T(8,128)(2,1)}, u32[]{:S(2)}) copy-start(bf16[32,64,512]{2,1,0:T(8,128)(2,1)} %values.1) | copy-start | bytes 6291460
  8.2 86.9 %copy-start.3 = (bf16[256,256]{1,0:T(8,128)(2,1)S(1)}, bf16[256,256]{1,0:T(8,128)(2,1)}, u32[]{:S(2)}) copy-start(bf16[256,256]{1,0:T(8,128)(2,1)} %w_self.3) | copy-start | bytes 393220
  8.2 87.0 %copy-start.4 = (bf16[256,256]{1,0:T(8,128)(2,1)S(1)}, bf16[256,256]{1,0:T(8,128)(2,1)}, u32[]{:S(2)}) copy-start(bf16[256,256]{1,0:T(8,128)(2,1)} %w_neigh.3) | copy-start | bytes 393220
  8.2 87.0 %copy-start.5 = (bf16[256,172]{0,1:T(8,128)(2,1)S(1)}, bf16[256,172]{0,1:T(8,128)(2,1)}, u32[]{:S(2)}) copy-start(bf16[256,172]{0,1:T(8,128)(2,1)} %param.28) | copy-start | bytes 264196
  8.2 87.0 %copy-start.9 = (f32[256]{0:T(256)S(1)}, f32[256]{0:T(256)}, u32[]{:S(2)}) copy-start(f32[256]{0:T(256)} %param.27) | copy-start | bytes 3076

commit v2 on v1

v2 whole, which is shorter than its diff:
```python
import functools

import jax
import jax.numpy as jnp
from jax import lax
from jax.experimental import pallas as pl
from jax.experimental.pallas import tpu as pltpu
from jax.sharding import PartitionSpec as P

MESH = pl.DeviceIdType.MESH
BLOCK = 64
GROUPS = 64
HALF_CAP = 256
FEAT = 128
HID = 256
TB = 64
OWN_TB = 32
NBR = 8
STORE = 16384
CHUNKS = 4
ROW_CHUNKS = 8


ORDER = (
    42, 54, 28, 4, 46, 61, 23, 34, 8, 59, 17, 6, 44, 45, 7, 50,
    24, 29, 55, 30, 52, 47, 5, 13, 39, 58, 16, 1, 43, 62, 20, 2,
    40, 41, 3, 15, 37, 18, 56, 63, 21, 11, 33, 48, 26, 12, 38, 36,
    14, 53, 31, 22, 60, 10, 32, 35, 9, 19, 57, 51, 25, 27, 49,
)
WORDS = [
    sum(s * 64**e for e, s in enumerate(ORDER[w : w + 5])) for w in range(0, GROUPS - 1, 5)
]


def shift_of(i):
    word = jnp.int32(WORDS[0])
    for w in range(1, len(WORDS)):
        word = jnp.where(i // 5 == w, jnp.int32(WORDS[w]), word)
    place = lax.rem(i, 5)
    shift = lax.rem(word, 64)
    for e in range(1, 5):
        shift = jnp.where(place == e, lax.rem(word // 64**e, 64), shift)
    return shift


def peer(me, s, c):
    z, y, x = me // 16, (me // 4) % 4, me % 4
    dz, dy, dx = s // 16, (s // 4) % 4, s % 4
    dz, dy, dx = (lax.rem(d * (1 + 2 * c), 4) for d in (dz, dy, dx))
    return ((z + dz) % 4) * 16 + ((y + dy) % 4) * 4 + (x + dx) % 4


def kernel(
    store_hbm,
    req_hbm,
    index_hbm,
    values_hbm,
    frontier,
    w_self_hbm,
    w_neigh_hbm,
    bias_hbm,
    index_two_hbm,
    values_two_hbm,
    w_self_two_hbm,
    w_neigh_two_hbm,
    bias_two_hbm,
    out,
    cols,
    rows,
    req,
    sreq,
    rreq,
    idx,
    index_vec,
    index,
    index_two,
    tmp,
    sendbuf,
    rbuf,
    values,
    values_two,
    held,
    w_self,
    w_neigh,
    bias,
    w_self_two,
    w_neigh_two,
    bias_two,
    psend,
    precv,
    totals,
    totals_two,
    selfbuf,
    agg,
    l1,
    pre_two,
    l2,
    load_sem,
    half_send,
    half_recv,
    req_send,
    req_recv,
    idx_sem,
    msg_send,
    msg_recv,
    p_send,
    p_recv,
    self_send,
    self_recv,
    self_own,
    l1_send,
    l1_recv,
    out_sem,
):
    me = lax.axis_index("batch")
    c = lax.axis_index("feat")
    sib = 1 - c
    f32, bf16 = jnp.float32, jnp.bfloat16

    barrier = pltpu.get_barrier_semaphore()
    pl.semaphore_signal(barrier, inc=1, device_id=(me, sib), device_id_type=MESH)

    def greet(s, _):
        pl.semaphore_signal(
            barrier, inc=1, device_id=(lax.rem(me + s, GROUPS), c), device_id_type=MESH
        )
        return 0

    lax.fori_loop(1, GROUPS, greet, 0)

    half = pl.ds(pl.multiple_of(c * 64, 64), 64)
    loads = [
        pltpu.make_async_copy(src, dst, load_sem.at[i])
        for i, (src, dst) in enumerate(
            (
                (req_hbm, req),
                (store_hbm, cols.at[half]),
                (index_hbm, index_vec),
                (index_hbm, index),
                (index_two_hbm, index_two),
                (w_self_hbm, w_self),
                (w_neigh_hbm, w_neigh),
                (bias_hbm, bias),
                (w_self_two_hbm, w_self_two),
                (w_neigh_two_hbm, w_neigh_two),
                (bias_two_hbm, bias_two),
                (values_hbm, values),
                (values_two_hbm, values_two),
            )
        )
    ]
    for load in loads:
        load.start()
    loads[0].wait()
    for h in range(2):
        sreq[:, h, :] = req[:, pl.ds(pl.multiple_of(c * HALF_CAP + h * 128, 128), 128)]
    rreq[me] = sreq[me]
    pl.semaphore_wait(barrier, GROUPS)

    def req_copy(s):
        p = lax.rem(me + s, GROUPS)
        return pltpu.make_async_remote_copy(
            src_ref=sreq.at[p],
            dst_ref=rreq.at[me],
            send_sem=req_send.at[s],
            recv_sem=req_recv.at[s],
            device_id=(p, c),
            device_id_type=MESH,
        )

    width = STORE // CHUNKS

    def half_copy(j):
        part = pl.ds(j * width, width)
        return pltpu.make_async_remote_copy(
            src_ref=store_hbm.at[:, part],
            dst_ref=cols.at[half, part],
            send_sem=half_send.at[j],
            recv_sem=half_recv.at[j],
            device_id=(me, sib),
            device_id_type=MESH,
        )

    half_copy(0).start()

    def req_start(s, _):
        req_copy(s).start()
        return 0

    lax.fori_loop(1, GROUPS, req_start, 0)
    for j in range(1, CHUNKS):
        half_copy(j).start()
    loads[1].wait()
    for j in range(CHUNKS):
        half_copy(j).wait_recv()
        part = pl.ds(j * width, width)
        rows[part, :] = cols[:, part].T.astype(f32)

    def req_wait(s, _):
        req_copy(s).wait_recv()
        return 0

    lax.fori_loop(1, GROUPS, req_wait, 0)
    idx_copy = pltpu.make_async_copy(rreq, idx, idx_sem)
    idx_copy.start()
    idx_copy.wait()

    def gather(p):
        for h in range(2):
            for q in range(128):
                tmp[pl.ds(h * 128 + q, 1), :] = rows[pl.ds(idx[p, h, q], 1), :]
        return tmp[...].astype(bf16).reshape(4, BLOCK, FEAT)

    def msg_copy(s):
        p = peer(me, s, c)
        return pltpu.make_async_remote_copy(
            src_ref=sendbuf.at[pl.ds(p * 4, 4)],
            dst_ref=rbuf.at[pl.ds(me * 4, 4)],
            send_sem=msg_send.at[s],
            recv_sem=msg_recv.at[s],
            device_id=(p, c),
            device_id_type=MESH,
        )

    def msg_start(i, _):
        s = shift_of(i)
        p = peer(me, s, c)
        sendbuf[pl.ds(p * 4, 4)] = gather(p)
        msg_copy(s).start()
        return 0

    lax.fori_loop(0, GROUPS - 1, msg_start, 0)
    rbuf[pl.ds(me * 4, 4)] = gather(me)

    for load in loads[2:]:
        load.wait()
    ones = jnp.ones((NBR * BLOCK, FEAT), bf16)

    def total(t, _):
        totals[t] = jnp.dot(values[c * OWN_TB + t], ones, preferred_element_type=f32)
        totals_two[t] = jnp.dot(values_two[t], ones, preferred_element_type=f32)
        return 0

    lax.fori_loop(0, OWN_TB, total, 0)
    spread = lax.broadcasted_iota(jnp.int32, (NBR, NBR * BLOCK), 1) // BLOCK
    spread = (spread == lax.broadcasted_iota(jnp.int32, (NBR, NBR * BLOCK), 0)).astype(f32)
    mine = (((index_vec[...] >> 2) & 1) == c).astype(f32)
    held[...] = lax.dot_general(
        mine, spread, (((0,), (0,)), ((), ())), preferred_element_type=f32
    )

    def mask(t, _):
        values[t] = values[t] * held[pl.ds(t, 1), :].astype(bf16)
        return 0

    lax.fori_loop(0, TB, mask, 0)

    def msg_wait(s, _):
        msg_copy(s).wait_recv()
        return 0

    lax.fori_loop(1, GROUPS, msg_wait, 0)

    def self_copy(j):
        return pltpu.make_async_remote_copy(
            src_ref=rbuf.at[pl.ds((sib * 4 + j) * 4, 4)],
            dst_ref=selfbuf.at[2 * j + c],
            send_sem=self_send.at[j],
            recv_sem=self_recv.at[j],
            device_id=(me, sib),
            device_id_type=MESH,
        )

    def self_local(j):
        return pltpu.make_async_copy(
            rbuf.at[pl.ds((c * 4 + j) * 4, 4)], selfbuf.at[2 * j + c], self_own.at[j]
        )

    for j in range(4):
        self_copy(j).start()
        self_local(j).start()

    def partial_sum(t):
        parts = []
        for k in range(NBR):
            b = index[k, t]
            parts.append(rbuf[(b >> 3) * 4 + (b & 3)])
        return jnp.dot(values[t], jnp.concatenate(parts, axis=0), preferred_element_type=f32)

    def p_copy(m):
        return pltpu.make_async_remote_copy(
            src_ref=psend.at[pl.ds(m * 8, 8)],
            dst_ref=precv.at[pl.ds(m * 8, 8)],
            send_sem=p_send.at[m],
            recv_sem=p_recv.at[m],
            device_id=(me, sib),
            device_id_type=MESH,
        )

    for m in range(4):
        for u in range(8):
            t = m * 8 + u
            psend[t] = partial_sum(sib * OWN_TB + t)
        p_copy(m).start()

    def own(i, _):
        for u in range(8):
            t = i * 8 + u
            agg[t] = partial_sum(c * OWN_TB + t)
        return 0

    lax.fori_loop(0, OWN_TB // 8, own, 0)

    def l1_copy(m):
        part = l1.at[pl.ds(c * OWN_TB + m * 4, 4)]
        return pltpu.make_async_remote_copy(
            src_ref=part,
            dst_ref=part,
            send_sem=l1_send.at[m],
            recv_sem=l1_recv.at[m],
            device_id=(me, sib),
            device_id_type=MESH,
        )

    def active(m):
        number = c * OWN_TB + m * 4 + lax.broadcasted_iota(jnp.int32, (256, HID), 0) // BLOCK
        return number < frontier[0]

    for j in range(4):
        self_copy(j).wait_recv()
        self_local(j).wait()
    for m in range(ROW_CHUNKS):
        if m % 2 == 0:
            p_copy(m // 2).wait_recv()
        mean = (agg[pl.ds(m * 4, 4)] + precv[pl.ds(m * 4, 4)]) / totals[pl.ds(m * 4, 4)]
        mean = mean.astype(bf16).reshape(256, FEAT)
        pre = (
            jnp.dot(selfbuf[m].reshape(256, FEAT), w_self[...], preferred_element_type=f32)
            + jnp.dot(mean, w_neigh[...], preferred_element_type=f32)
            + bias[...]
        )
        layer = jnp.where(active(m), jnp.maximum(pre, 0.0), 0.0).astype(bf16)
        l1[pl.ds(c * OWN_TB + m * 4, 4)] = layer.reshape(4, BLOCK, HID)
        l1_copy(m).start()

    def own_part(m, _):
        mine = l1[pl.ds(c * OWN_TB + m * 4, 4)].reshape(256, HID)
        pre_two[pl.ds(m * 4, 4)] = (
            jnp.dot(mine, w_self_two[...], preferred_element_type=f32) + bias_two[...]
        ).reshape(4, BLOCK, HID)
        return 0

    lax.fori_loop(0, ROW_CHUNKS, own_part, 0)
    for m in range(ROW_CHUNKS):
        l1_copy(m).wait_recv()

    def out_copy(m):
        at = pl.ds(m * 256, 256)
        return pltpu.make_async_copy(l2.at[at], out.at[at], out_sem.at[m])

    for m in range(ROW_CHUNKS):
        means = []
        for u in range(4):
            t = m * 4 + u
            parts = [l1[index_two[k, t]] for k in range(NBR)]
            summed = jnp.dot(
                values_two[t], jnp.concatenate(parts, axis=0), preferred_element_type=f32
            )
            total = jnp.concatenate([totals_two[t], totals_two[t]], axis=1)
            means.append((summed / total).astype(bf16))
        mean = jnp.concatenate(means, axis=0)
        pre = (
            jnp.dot(mean, w_neigh_two[...], preferred_element_type=f32)
            + pre_two[pl.ds(m * 4, 4)].reshape(256, HID)
        )
        layer = jnp.where(active(m), jnp.maximum(pre, 0.0), 0.0)
        l2[pl.ds(m * 256, 256), :] = layer.astype(bf16)
        out_copy(m).start()

    for m in range(ROW_CHUNKS):
        out_copy(m).wait()
        l1_copy(m).wait_send()
    for j in range(CHUNKS):
        half_copy(j).wait_send()
    for j in range(4):
        self_copy(j).wait_send()
        p_copy(j).wait_send()

    def sent(s, _):
        req_copy(s).wait_send()
        msg_copy(s).wait_send()
        return 0

    lax.fori_loop(1, GROUPS, sent, 0)


def body(
    feature_store,
    requests,
    block_index,
    block_values,
    frontier,
    self_first,
    neigh_first,
    bias_first,
    second_index,
    second_values,
    self_second,
    neigh_second,
    bias_second,
    classifier,
    bias_class,
):
    smem = pl.BlockSpec(memory_space=pltpu.SMEM)
    hbm = pl.BlockSpec(memory_space=pl.ANY)
    dma = pltpu.SemaphoreType.DMA
    bf16, f32, i32 = jnp.bfloat16, jnp.float32, jnp.int32
    layer_two = pl.pallas_call(
        kernel,
        out_shape=jax.ShapeDtypeStruct((OWN_TB * BLOCK, HID), bf16),
        in_specs=[hbm] * 4 + [smem] + [hbm] * 8,
        out_specs=hbm,
        scratch_shapes=[
            pltpu.VMEM((FEAT, STORE), bf16),
            pltpu.VMEM((STORE, FEAT), f32),
            pltpu.VMEM((GROUPS, 2 * HALF_CAP), i32),
            pltpu.VMEM((GROUPS, 2, 128), i32),
            pltpu.VMEM((GROUPS, 2, 128), i32),
            pltpu.SMEM((GROUPS, 2, 128), i32),
            pltpu.VMEM((NBR, TB), i32),
            pltpu.SMEM((NBR, TB), i32),
            pltpu.SMEM((NBR, OWN_TB), i32),
            pltpu.VMEM((HALF_CAP, FEAT), f32),
            pltpu.VMEM((GROUPS * 4, BLOCK, FEAT), bf16),
            pltpu.VMEM((GROUPS * 4, BLOCK, FEAT), bf16),
            pltpu.VMEM((TB, BLOCK, NBR * BLOCK), bf16),
            pltpu.VMEM((OWN_TB, BLOCK, NBR * BLOCK), bf16),
            pltpu.VMEM((TB, NBR * BLOCK), f32),
            pltpu.VMEM((FEAT, HID), bf16),
            pltpu.VMEM((FEAT, HID), bf16),
            pltpu.VMEM((1, HID), f32),
            pltpu.VMEM((HID, HID), bf16),
            pltpu.VMEM((HID, HID), bf16),
            pltpu.VMEM((1, HID), f32),
            pltpu.VMEM((OWN_TB, BLOCK, FEAT), f32),
            pltpu.VMEM((OWN_TB, BLOCK, FEAT), f32),
            pltpu.VMEM((OWN_TB, BLOCK, FEAT), f32),
            pltpu.VMEM((OWN_TB, BLOCK, FEAT), f32),
            pltpu.VMEM((8, 4, BLOCK, FEAT), bf16),
            pltpu.VMEM((OWN_TB, BLOCK, FEAT), f32),
            pltpu.VMEM((TB, BLOCK, HID), bf16),
            pltpu.VMEM((OWN_TB, BLOCK, HID), f32),
            pltpu.VMEM((OWN_TB * BLOCK, HID), bf16),
            dma((13,)),
            dma((CHUNKS,)),
            dma((CHUNKS,)),
            dma((GROUPS,)),
            dma((GROUPS,)),
            dma,
            dma((GROUPS,)),
            dma((GROUPS,)),
            dma((4,)),
            dma((4,)),
            dma((4,)),
            dma((4,)),
            dma((4,)),
            dma((ROW_CHUNKS,)),
            dma((ROW_CHUNKS,)),
            dma((ROW_CHUNKS,)),
        ],
        compiler_params=pltpu.CompilerParams(
            collective_id=0, has_side_effects=True, vmem_limit_bytes=60 * 2**20
        ),
        name="graph_layers",
    )(
        feature_store,
        requests,
        block_index.T,
        block_values,
        frontier,
        self_first,
        neigh_first,
        bias_first.reshape(1, HID),
        second_index.T,
        second_values,
        self_second,
        neigh_second,
        bias_second.reshape(1, HID),
    )
    return jnp.dot(layer_two, classifier, preferred_element_type=f32) + bias_class


def solution(mesh):
    in_specs = (
        P("feat", "batch"),
        P("batch", None),
        P("batch", None),
        P("batch", None, None),
        P("batch"),
        P(),
        P(),
        P(),
        P(("batch", "feat"), None),
        P(("batch", "feat"), None, None),
        P(),
        P(),
        P(),
        P(),
        P(),
    )
    out_specs = P(("batch", "feat"), None)
    return jax.shard_map(body, mesh=mesh, in_specs=in_specs, out_specs=out_specs, check_vma=False)
```

time: 104 us -> 84.1 us (0.81)
  Pallas kernels: 94.9 us -> 80.2 us
  local copies, waits for them, and re-layouts: 7.43 us -> 0.01 us
  matrix products: 0 us -> 2.83 us
    pallas_call x2 -> x1, Pallas kernels: 94.9 us -> 80.2 us  [body(): pl.pallas_call(kernel, out_shape=jax.ShapeDtypeStruct((OWN_TB * BLOCK, HI...]
    unnamed x22 -> x4, local copies, waits for them, and re-layouts: 6.4 us -> 0.01 us
    dot_general x0 -> x1, matrix products: none -> 2.83 us  [body(): jnp.dot(layer_two, classifier, preferred_element_type=f32) + bias_class]
where the time goes in v2:
time: 84.1 us; the launch traced here: 83.8 us
  Pallas kernels  80.2 us (95%)
  matrix products  2.83 us (3%)
    pallas_call x1, Pallas kernels, body(): pl.pallas_call(kernel, out_shape=jax.ShapeDtypeStruct((OWN_TB * BLOCK, HI...  80.2 us
    dot_general x1, matrix products, body(): jnp.dot(layer_two, classifier, preferred_element_type=f32) + bias_class  2.83 us

profile of v2, /device:TPU:1, one launch (start us, length us, event | category | flops | bytes accessed | tf_op | source)
XLA Modules:
  0.0 83.8 jit_solution(7175479130366047738)
XLA Ops:
  0.0 0.0 copy-start
  0.7 0.0 copy-start.1
  0.7 80.2 %graph_layers.1 = bf16[2048,256]{1,0:T(8,128)(2,1)} custom-call(bf16[64,16384]{1,0:T(8,128)(2,1)} %store_hbm.1, s32[64,512]{1,0:T(8,128)} %req_hbm.1, s32[8,64]{1,0:T(8,128)} %bitcast.6, bf16[64,64,512]{2,1,0:T(8,128)(2,1)} %values_hbm.1, s32[1]{0:T(128)S(6)} %copy.16.frontier, bf16[128,256]{1,0:T(8,128)(2,1)} %w_self_hbm.1, bf16[128,256]{1,0:T(8,128)(2,1)} %w_neigh_hbm.1, ...), custom_call_target="tpu_custom_call" | custom-call | tf_op jit(solution)/shard_map/graph_layers/pallas_call | solution.py:418
  80.9 0.0 copy-done
  80.9 0.0 copy-done.1
  81.0 2.8 %convolution_add_fusion = f32[2048,172]{0,1:T(8,128)} fusion(bf16[2048,256]{1,0:T(8,128)(2,1)} %graph_layers.1, bf16[256,172]{0,1:T(8,128)(2,1)S(1)} %copy-done, f32[172]{0:T(256)S(1)} %copy-done.1), kind=kOutput, calls=%fused_computation | convolution fusion | flops 180707328 | bytes 2546352 | tf_op jit(solution)/shard_map/dot_general | solution.py:490
Async XLA Ops:
  0.0 80.9 %copy-start = (bf16[256,172]{0,1:T(8,128)(2,1)S(1)}, bf16[256,172]{0,1:T(8,128)(2,1)}, u32[]{:S(2)}) copy-start(bf16[256,172]{0,1:T(8,128)(2,1)} %param.28) | copy-start | bytes 264196
  0.7 80.3 %copy-start.1 = (f32[172]{0:T(256)S(1)}, f32[172]{0:T(256)}, u32[]{:S(2)}) copy-start(f32[172]{0:T(256)} %param.29) | copy-start | bytes 2068

commit v3 on v2

--- a/solution.py
+++ b/solution.py
@@ -80,8 +80,7 @@
     values,
     values_two,
     held,
-    w_self,
-    w_neigh,
+    w_first,
     bias,
     w_self_two,
     w_neigh_two,
@@ -95,6 +94,8 @@
     l1,
     pre_two,
     l2,
+    req_sem,
+    own_sem,
     load_sem,
     half_send,
     half_recv,
@@ -117,6 +118,11 @@
     sib = 1 - c
     f32, bf16 = jnp.float32, jnp.bfloat16
 
+    half = pl.ds(pl.multiple_of(c * 64, 64), 64)
+    req_load = pltpu.make_async_copy(req_hbm, req, req_sem)
+    req_load.start()
+    own_load = pltpu.make_async_copy(store_hbm, cols.at[half], own_sem)
+    own_load.start()
     barrier = pltpu.get_barrier_semaphore()
     pl.semaphore_signal(barrier, inc=1, device_id=(me, sib), device_id_type=MESH)
 
@@ -128,18 +134,15 @@
 
     lax.fori_loop(1, GROUPS, greet, 0)
 
-    half = pl.ds(pl.multiple_of(c * 64, 64), 64)
     loads = [
         pltpu.make_async_copy(src, dst, load_sem.at[i])
         for i, (src, dst) in enumerate(
             (
-                (req_hbm, req),
-                (store_hbm, cols.at[half]),
                 (index_hbm, index_vec),
                 (index_hbm, index),
                 (index_two_hbm, index_two),
-                (w_self_hbm, w_self),
-                (w_neigh_hbm, w_neigh),
+                (w_self_hbm, w_first.at[pl.ds(0, FEAT)]),
+                (w_neigh_hbm, w_first.at[pl.ds(FEAT, FEAT)]),
                 (bias_hbm, bias),
                 (w_self_two_hbm, w_self_two),
                 (w_neigh_two_hbm, w_neigh_two),
@@ -149,9 +152,7 @@
             )
         )
     ]
-    for load in loads:
-        load.start()
-    loads[0].wait()
+    req_load.wait()
     for h in range(2):
         sreq[:, h, :] = req[:, pl.ds(pl.multiple_of(c * HALF_CAP + h * 128, 128), 128)]
     rreq[me] = sreq[me]
@@ -162,8 +163,8 @@
         return pltpu.make_async_remote_copy(
             src_ref=sreq.at[p],
             dst_ref=rreq.at[me],
-            send_sem=req_send.at[s],
-            recv_sem=req_recv.at[s],
+            send_sem=req_send,
+            recv_sem=req_recv,
             device_id=(p, c),
             device_id_type=MESH,
         )
@@ -190,19 +191,22 @@
     lax.fori_loop(1, GROUPS, req_start, 0)
     for j in range(1, CHUNKS):
         half_copy(j).start()
-    loads[1].wait()
+    own_load.wait()
+    for load in loads:
+        load.start()
+
+    def wait_all(ref, rows_in_all, sem):
+        part = ref.at[pl.ds(0, rows_in_all)]
+        pltpu.make_async_copy(part, part, sem).wait()
+
+    idx_copy = pltpu.make_async_copy(rreq, idx, idx_sem)
     for j in range(CHUNKS):
         half_copy(j).wait_recv()
         part = pl.ds(j * width, width)
         rows[part, :] = cols[:, part].T.astype(f32)
-
-    def req_wait(s, _):
-        req_copy(s).wait_recv()
-        return 0
-
-    lax.fori_loop(1, GROUPS, req_wait, 0)
-    idx_copy = pltpu.make_async_copy(rreq, idx, idx_sem)
-    idx_copy.start()
+        if j == CHUNKS - 2:
+            wait_all(rreq, GROUPS - 1, req_recv)
+            idx_copy.start()
     idx_copy.wait()
 
     def gather(p):
@@ -216,8 +220,8 @@
         return pltpu.make_async_remote_copy(
             src_ref=sendbuf.at[pl.ds(p * 4, 4)],
             dst_ref=rbuf.at[pl.ds(me * 4, 4)],
-            send_sem=msg_send.at[s],
-            recv_sem=msg_recv.at[s],
+            send_sem=msg_send,
+            recv_sem=msg_recv,
             device_id=(p, c),
             device_id_type=MESH,
         )
@@ -232,7 +236,7 @@
     lax.fori_loop(0, GROUPS - 1, msg_start, 0)
     rbuf[pl.ds(me * 4, 4)] = gather(me)
 
-    for load in loads[2:]:
+    for load in loads:
         load.wait()
     ones = jnp.ones((NBR * BLOCK, FEAT), bf16)
 
@@ -254,12 +258,10 @@
         return 0
 
     lax.fori_loop(0, TB, mask, 0)
-
-    def msg_wait(s, _):
-        msg_copy(s).wait_recv()
-        return 0
-
-    lax.fori_loop(1, GROUPS, msg_wait, 0)
+    wait_all(sreq, GROUPS - 1, req_send)
+    for j in range(CHUNKS):
+        half_copy(j).wait_send()
+    wait_all(rbuf, (GROUPS - 1) * 4, msg_recv)
 
     def self_copy(j):
         return pltpu.make_async_remote_copy(
@@ -280,12 +282,20 @@
         self_copy(j).start()
         self_local(j).start()
 
-    def partial_sum(t):
-        parts = []
-        for k in range(NBR):
-            b = index[k, t]
-            parts.append(rbuf[(b >> 3) * 4 + (b & 3)])
-        return jnp.dot(values[t], jnp.concatenate(parts, axis=0), preferred_element_type=f32)
+    def partial_sums(t):
+        both = []
+        for u in range(2):
+            parts = []
+            for k in range(NBR):
+                b = index[k, t + u]
+                parts.append(rbuf[(b >> 3) * 4 + (b & 3)])
+            both.append(jnp.concatenate(parts, axis=0))
+        product = jnp.dot(
+            values[pl.ds(t, 2)].reshape(2 * BLOCK, NBR * BLOCK),
+            jnp.concatenate(both, axis=1),
+            preferred_element_type=f32,
+        )
+        return product[:BLOCK, :FEAT], product[BLOCK:, FEAT:]
 
     def p_copy(m):
         return pltpu.make_async_remote_copy(
@@ -298,15 +308,14 @@
         )
 
     for m in range(4):
-        for u in range(8):
-            t = m * 8 + u
-            psend[t] = partial_sum(sib * OWN_TB + t)
+        for t in range(m * 8, m * 8 + 8, 2):
+            psend[t], psend[t + 1] = partial_sums(sib * OWN_TB + t)
         p_copy(m).start()
 
     def own(i, _):
-        for u in range(8):
+        for u in range(0, 8, 2):
             t = i * 8 + u
-            agg[t] = partial_sum(c * OWN_TB + t)
+            agg[t], agg[t + 1] = partial_sums(c * OWN_TB + t)
         return 0
 
     lax.fori_loop(0, OWN_TB // 8, own, 0)
@@ -334,11 +343,8 @@
             p_copy(m // 2).wait_recv()
         mean = (agg[pl.ds(m * 4, 4)] + precv[pl.ds(m * 4, 4)]) / totals[pl.ds(m * 4, 4)]
         mean = mean.astype(bf16).reshape(256, FEAT)
-        pre = (
-            jnp.dot(selfbuf[m].reshape(256, FEAT), w_self[...], preferred_element_type=f32)
-            + jnp.dot(mean, w_neigh[...], preferred_element_type=f32)
-            + bias[...]
-        )
+        both = jnp.concatenate([selfbuf[m].reshape(256, FEAT), mean], axis=1)
+        pre = jnp.dot(both, w_first[...], preferred_element_type=f32) + bias[...]
         layer = jnp.where(active(m), jnp.maximum(pre, 0.0), 0.0).astype(bf16)
         l1[pl.ds(c * OWN_TB + m * 4, 4)] = layer.reshape(4, BLOCK, HID)
         l1_copy(m).start()
@@ -380,18 +386,10 @@
     for m in range(ROW_CHUNKS):
         out_copy(m).wait()
         l1_copy(m).wait_send()
-    for j in range(CHUNKS):
-        half_copy(j).wait_send()
     for j in range(4):
         self_copy(j).wait_send()
         p_copy(j).wait_send()
-
-    def sent(s, _):
-        req_copy(s).wait_send()
-        msg_copy(s).wait_send()
-        return 0
-
-    lax.fori_loop(1, GROUPS, sent, 0)
+    wait_all(sendbuf, (GROUPS - 1) * 4, msg_send)
 
 
 def body(
@@ -436,8 +434,7 @@
             pltpu.VMEM((TB, BLOCK, NBR * BLOCK), bf16),
             pltpu.VMEM((OWN_TB, BLOCK, NBR * BLOCK), bf16),
             pltpu.VMEM((TB, NBR * BLOCK), f32),
-            pltpu.VMEM((FEAT, HID), bf16),
-            pltpu.VMEM((FEAT, HID), bf16),
+            pltpu.VMEM((2 * FEAT, HID), bf16),
             pltpu.VMEM((1, HID), f32),
             pltpu.VMEM((HID, HID), bf16),
             pltpu.VMEM((HID, HID), bf16),
@@ -451,14 +448,16 @@
             pltpu.VMEM((TB, BLOCK, HID), bf16),
             pltpu.VMEM((OWN_TB, BLOCK, HID), f32),
             pltpu.VMEM((OWN_TB * BLOCK, HID), bf16),
-            dma((13,)),
+            dma,
+            dma,
+            dma((11,)),
             dma((CHUNKS,)),
             dma((CHUNKS,)),
-            dma((GROUPS,)),
-            dma((GROUPS,)),
-            dma,
-            dma((GROUPS,)),
-            dma((GROUPS,)),
+            dma,
+            dma,
+            dma,
+            dma,
+            dma,
             dma((4,)),
             dma((4,)),
             dma((4,)),

time: 84.1 us -> 80.4 us (0.956)
  Pallas kernels: 80.2 us -> 76.7 us
    pallas_call x1, Pallas kernels: 80.2 us -> 76.7 us  [body(): pl.pallas_call(kernel, out_shape=jax.ShapeDtypeStruct((OWN_TB * BLOCK, HI...]
where the time goes in v3:
time: 80.4 us; the launch traced here: 80.3 us
  Pallas kernels  76.7 us (95%)
  matrix products  2.83 us (4%)
    pallas_call x1, Pallas kernels, body(): pl.pallas_call(kernel, out_shape=jax.ShapeDtypeStruct((OWN_TB * BLOCK, HI...  76.7 us
    dot_general x1, matrix products, body(): jnp.dot(layer_two, classifier, preferred_element_type=f32) + bias_class  2.83 us

profile of v3, /device:TPU:1, one launch (start us, length us, event | category | flops | bytes accessed | tf_op | source)
XLA Modules:
  0.0 80.3 jit_solution(18024227820457153180)
XLA Ops:
  0.0 0.0 copy-start
  0.7 0.0 copy-start.1
  0.7 76.7 %graph_layers.1 = bf16[2048,256]{1,0:T(8,128)(2,1)} custom-call(bf16[64,16384]{1,0:T(8,128)(2,1)} %store_hbm.1, s32[64,512]{1,0:T(8,128)} %req_hbm.1, s32[8,64]{1,0:T(8,128)} %bitcast.6, bf16[64,64,512]{2,1,0:T(8,128)(2,1)} %values_hbm.1, s32[1]{0:T(128)S(6)} %copy.16.frontier, bf16[128,256]{1,0:T(8,128)(2,1)} %w_self_hbm.1, bf16[128,256]{1,0:T(8,128)(2,1)} %w_neigh_hbm.1, ...), custom_call_target="tpu_custom_call" | custom-call | tf_op jit(solution)/shard_map/graph_layers/pallas_call | solution.py:416
  77.4 0.0 copy-done
  77.4 0.0 copy-done.1
  77.4 2.8 %convolution_add_fusion = f32[2048,172]{0,1:T(8,128)} fusion(bf16[2048,256]{1,0:T(8,128)(2,1)} %graph_layers.1, bf16[256,172]{0,1:T(8,128)(2,1)S(1)} %copy-done, f32[172]{0:T(256)S(1)} %copy-done.1), kind=kOutput, calls=%fused_computation | convolution fusion | flops 180707328 | bytes 2546352 | tf_op jit(solution)/shard_map/dot_general | solution.py:489
Async XLA Ops:
  0.0 77.4 %copy-start = (bf16[256,172]{0,1:T(8,128)(2,1)S(1)}, bf16[256,172]{0,1:T(8,128)(2,1)}, u32[]{:S(2)}) copy-start(bf16[256,172]{0,1:T(8,128)(2,1)} %param.28) | copy-start | bytes 264196
  0.7 76.7 %copy-start.1 = (f32[172]{0:T(256)S(1)}, f32[172]{0:T(256)}, u32[]{:S(2)}) copy-start(f32[172]{0:T(256)} %param.29) | copy-start | bytes 2068

commit v4 on v3

--- a/solution.py
+++ b/solution.py
@@ -93,7 +93,6 @@
     agg,
     l1,
     pre_two,
-    l2,
     req_sem,
     own_sem,
     load_sem,
@@ -108,10 +107,8 @@
     p_recv,
     self_send,
     self_recv,
-    self_own,
     l1_send,
     l1_recv,
-    out_sem,
 ):
     me = lax.axis_index("batch")
     c = lax.axis_index("feat")
@@ -273,14 +270,11 @@
             device_id_type=MESH,
         )
 
-    def self_local(j):
-        return pltpu.make_async_copy(
-            rbuf.at[pl.ds((c * 4 + j) * 4, 4)], selfbuf.at[2 * j + c], self_own.at[j]
-        )
-
     for j in range(4):
         self_copy(j).start()
-        self_local(j).start()
+
+    for j in range(4):
+        selfbuf[2 * j + c] = rbuf[pl.ds((c * 4 + j) * 4, 4)]
 
     def partial_sums(t):
         both = []
@@ -337,7 +331,6 @@
 
     for j in range(4):
         self_copy(j).wait_recv()
-        self_local(j).wait()
     for m in range(ROW_CHUNKS):
         if m % 2 == 0:
             p_copy(m // 2).wait_recv()
@@ -359,10 +352,6 @@
     lax.fori_loop(0, ROW_CHUNKS, own_part, 0)
     for m in range(ROW_CHUNKS):
         l1_copy(m).wait_recv()
-
-    def out_copy(m):
-        at = pl.ds(m * 256, 256)
-        return pltpu.make_async_copy(l2.at[at], out.at[at], out_sem.at[m])
 
     for m in range(ROW_CHUNKS):
         means = []
@@ -380,11 +369,9 @@
             + pre_two[pl.ds(m * 4, 4)].reshape(256, HID)
         )
         layer = jnp.where(active(m), jnp.maximum(pre, 0.0), 0.0)
-        l2[pl.ds(m * 256, 256), :] = layer.astype(bf16)
-        out_copy(m).start()
+        out[pl.ds(m * 256, 256), :] = layer.astype(bf16)
 
     for m in range(ROW_CHUNKS):
-        out_copy(m).wait()
         l1_copy(m).wait_send()
     for j in range(4):
         self_copy(j).wait_send()
@@ -415,9 +402,9 @@
     bf16, f32, i32 = jnp.bfloat16, jnp.float32, jnp.int32
     layer_two = pl.pallas_call(
         kernel,
-        out_shape=jax.ShapeDtypeStruct((OWN_TB * BLOCK, HID), bf16),
+        out_shape=pltpu.VMEM((OWN_TB * BLOCK, HID), bf16),
         in_specs=[hbm] * 4 + [smem] + [hbm] * 8,
-        out_specs=hbm,
+        out_specs=pl.BlockSpec(memory_space=pltpu.VMEM),
         scratch_shapes=[
             pltpu.VMEM((FEAT, STORE), bf16),
             pltpu.VMEM((STORE, FEAT), f32),
@@ -447,7 +434,6 @@
             pltpu.VMEM((OWN_TB, BLOCK, FEAT), f32),
             pltpu.VMEM((TB, BLOCK, HID), bf16),
             pltpu.VMEM((OWN_TB, BLOCK, HID), f32),
-            pltpu.VMEM((OWN_TB * BLOCK, HID), bf16),
             dma,
             dma,
             dma((11,)),
@@ -458,17 +444,15 @@
             dma,
             dma,
             dma,
-            dma((4,)),
             dma((4,)),
             dma((4,)),
             dma((4,)),
             dma((4,)),
             dma((ROW_CHUNKS,)),
             dma((ROW_CHUNKS,)),
-            dma((ROW_CHUNKS,)),
         ],
         compiler_params=pltpu.CompilerParams(
-            collective_id=0, has_side_effects=True, vmem_limit_bytes=60 * 2**20
+            collective_id=0, has_side_effects=True, vmem_limit_bytes=58 * 2**20
         ),
         name="graph_layers",
     )(

time: 80.4 us -> 78.2 us (0.973)
  matrix products: 2.83 us -> 1.6 us
  Pallas kernels: 76.7 us -> 75.8 us
    dot_general x1, matrix products: 2.83 us -> 1.6 us  [body(): jnp.dot(layer_two, classifier, preferred_element_type=f32) + bias_class]
    pallas_call x1, Pallas kernels: 76.7 us -> 75.8 us  [body(): pl.pallas_call(kernel, out_shape=pltpu.VMEM((OWN_TB * BLOCK, HID), bf16),...]
where the time goes in v4:
time: 78.2 us; the launch traced here: 78.1 us
  Pallas kernels  75.8 us (97%)
  matrix products  1.6 us (2%)
    pallas_call x1, Pallas kernels, body(): pl.pallas_call(kernel, out_shape=pltpu.VMEM((OWN_TB * BLOCK, HID), bf16),...  75.8 us
    dot_general x1, matrix products, body(): jnp.dot(layer_two, classifier, preferred_element_type=f32) + bias_class  1.6 us

profile of v4, /device:TPU:1, one launch (start us, length us, event | category | flops | bytes accessed | tf_op | source)
XLA Modules:
  0.0 78.1 jit_solution(9989084992612030537)
XLA Ops:
  0.0 0.0 copy-start
  0.7 0.0 copy-start.1
  0.7 75.8 %graph_layers.1 = bf16[2048,256]{1,0:T(8,128)(2,1)S(1)} custom-call(bf16[64,16384]{1,0:T(8,128)(2,1)} %store_hbm.1, s32[64,512]{1,0:T(8,128)} %req_hbm.1, s32[8,64]{1,0:T(8,128)} %bitcast.6, bf16[64,64,512]{2,1,0:T(8,128)(2,1)} %values_hbm.1, s32[1]{0:T(128)S(6)} %copy.16.frontier, bf16[128,256]{1,0:T(8,128)(2,1)} %w_self_hbm.1, ...), custom_call_target="tpu_custom_call" | custom-call | tf_op jit(solution)/shard_map/graph_layers/pallas_call | solution.py:403
  76.5 0.0 copy-done
  76.5 0.0 copy-done.1
  76.5 1.6 %convolution_add_fusion = f32[2048,172]{0,1:T(8,128)} fusion(bf16[2048,256]{1,0:T(8,128)(2,1)S(1)} %graph_layers.1, bf16[256,172]{0,1:T(8,128)(2,1)S(1)} %copy-done, f32[172]{0:T(256)S(1)} %copy-done.1), kind=kOutput, calls=%fused_computation | convolution fusion | flops 180707328 | bytes 2546352 | tf_op jit(solution)/shard_map/dot_general | solution.py:473
Async XLA Ops:
  0.0 76.5 %copy-start = (bf16[256,172]{0,1:T(8,128)(2,1)S(1)}, bf16[256,172]{0,1:T(8,128)(2,1)}, u32[]{:S(2)}) copy-start(bf16[256,172]{0,1:T(8,128)(2,1)} %param.28) | copy-start | bytes 264196
  0.7 75.8 %copy-start.1 = (f32[172]{0:T(256)S(1)}, f32[172]{0:T(256)}, u32[]{:S(2)}) copy-start(f32[172]{0:T(256)} %param.29) | copy-start | bytes 2068

commit v5 on v4

--- a/solution.py
+++ b/solution.py
@@ -19,13 +19,16 @@
 STORE = 16384
 CHUNKS = 4
 ROW_CHUNKS = 8
+PARTS = 4
+PART_TB = OWN_TB // PARTS
+PART_ROWS = PART_TB * BLOCK
 
 
 ORDER = (
-    42, 54, 28, 4, 46, 61, 23, 34, 8, 59, 17, 6, 44, 45, 7, 50,
-    24, 29, 55, 30, 52, 47, 5, 13, 39, 58, 16, 1, 43, 62, 20, 2,
-    40, 41, 3, 15, 37, 18, 56, 63, 21, 11, 33, 48, 26, 12, 38, 36,
-    14, 53, 31, 22, 60, 10, 32, 35, 9, 19, 57, 51, 25, 27, 49,
+    42, 41, 2, 43, 46, 52, 26, 58, 20, 34, 60, 27, 49, 10, 17, 59,
+    19, 45, 5, 39, 15, 40, 13, 38, 62, 23, 57, 28, 54, 32, 25, 51,
+    22, 8, 47, 18, 56, 9, 33, 7, 30, 63, 37, 11, 29, 53, 35, 50,
+    24, 21, 44, 14, 55, 36, 31, 6, 61, 16, 4, 1, 12, 48, 3,
 )
 WORDS = [
     sum(s * 64**e for e, s in enumerate(ORDER[w : w + 5])) for w in range(0, GROUPS - 1, 5)
@@ -55,7 +58,7 @@
     req_hbm,
     index_hbm,
     values_hbm,
-    frontier,
+    frontier_hbm,
     w_self_hbm,
     w_neigh_hbm,
     bias_hbm,
@@ -74,6 +77,7 @@
     index_vec,
     index,
     index_two,
+    frontier,
     tmp,
     sendbuf,
     rbuf,
@@ -138,6 +142,7 @@
                 (index_hbm, index_vec),
                 (index_hbm, index),
                 (index_two_hbm, index_two),
+                (frontier_hbm, frontier),
                 (w_self_hbm, w_first.at[pl.ds(0, FEAT)]),
                 (w_neigh_hbm, w_first.at[pl.ds(FEAT, FEAT)]),
                 (bias_hbm, bias),
@@ -315,7 +320,7 @@
     lax.fori_loop(0, OWN_TB // 8, own, 0)
 
     def l1_copy(m):
-        part = l1.at[pl.ds(c * OWN_TB + m * 4, 4)]
+        part = l1.at[pl.ds(c * OWN_TB + m * PART_TB, PART_TB)]
         return pltpu.make_async_remote_copy(
             src_ref=part,
             dst_ref=part,
@@ -325,21 +330,22 @@
             device_id_type=MESH,
         )
 
-    def active(m):
-        number = c * OWN_TB + m * 4 + lax.broadcasted_iota(jnp.int32, (256, HID), 0) // BLOCK
-        return number < frontier[0]
+    def active(first, count):
+        rows_here = lax.broadcasted_iota(jnp.int32, (count * BLOCK, HID), 0) // BLOCK
+        return c * OWN_TB + first + rows_here < frontier[0]
 
     for j in range(4):
         self_copy(j).wait_recv()
-    for m in range(ROW_CHUNKS):
-        if m % 2 == 0:
-            p_copy(m // 2).wait_recv()
-        mean = (agg[pl.ds(m * 4, 4)] + precv[pl.ds(m * 4, 4)]) / totals[pl.ds(m * 4, 4)]
-        mean = mean.astype(bf16).reshape(256, FEAT)
-        both = jnp.concatenate([selfbuf[m].reshape(256, FEAT), mean], axis=1)
+    for m in range(PARTS):
+        for j in range(m * 4 // PARTS, (m + 1) * 4 // PARTS):
+            p_copy(j).wait_recv()
+        part = pl.ds(m * PART_TB, PART_TB)
+        mean = ((agg[part] + precv[part]) / totals[part]).astype(bf16).reshape(PART_ROWS, FEAT)
+        mine = selfbuf[pl.ds(m * 8 // PARTS, 8 // PARTS)].reshape(PART_ROWS, FEAT)
+        both = jnp.concatenate([mine, mean], axis=1)
         pre = jnp.dot(both, w_first[...], preferred_element_type=f32) + bias[...]
-        layer = jnp.where(active(m), jnp.maximum(pre, 0.0), 0.0).astype(bf16)
-        l1[pl.ds(c * OWN_TB + m * 4, 4)] = layer.reshape(4, BLOCK, HID)
+        layer = jnp.where(active(m * PART_TB, PART_TB), jnp.maximum(pre, 0.0), 0.0).astype(bf16)
+        l1[pl.ds(c * OWN_TB + m * PART_TB, PART_TB)] = layer.reshape(PART_TB, BLOCK, HID)
         l1_copy(m).start()
 
     def own_part(m, _):
@@ -350,7 +356,7 @@
         return 0
 
     lax.fori_loop(0, ROW_CHUNKS, own_part, 0)
-    for m in range(ROW_CHUNKS):
+    for m in range(PARTS):
         l1_copy(m).wait_recv()
 
     for m in range(ROW_CHUNKS):
@@ -368,10 +374,10 @@
             jnp.dot(mean, w_neigh_two[...], preferred_element_type=f32)
             + pre_two[pl.ds(m * 4, 4)].reshape(256, HID)
         )
-        layer = jnp.where(active(m), jnp.maximum(pre, 0.0), 0.0)
+        layer = jnp.where(active(m * 4, 4), jnp.maximum(pre, 0.0), 0.0)
         out[pl.ds(m * 256, 256), :] = layer.astype(bf16)
 
-    for m in range(ROW_CHUNKS):
+    for m in range(PARTS):
         l1_copy(m).wait_send()
     for j in range(4):
         self_copy(j).wait_send()
@@ -396,14 +402,13 @@
     classifier,
     bias_class,
 ):
-    smem = pl.BlockSpec(memory_space=pltpu.SMEM)
     hbm = pl.BlockSpec(memory_space=pl.ANY)
     dma = pltpu.SemaphoreType.DMA
     bf16, f32, i32 = jnp.bfloat16, jnp.float32, jnp.int32
     layer_two = pl.pallas_call(
         kernel,
         out_shape=pltpu.VMEM((OWN_TB * BLOCK, HID), bf16),
-        in_specs=[hbm] * 4 + [smem] + [hbm] * 8,
+        in_specs=[hbm] * 13,
         out_specs=pl.BlockSpec(memory_space=pltpu.VMEM),
         scratch_shapes=[
             pltpu.VMEM((FEAT, STORE), bf16),
@@ -415,6 +420,7 @@
             pltpu.VMEM((NBR, TB), i32),
             pltpu.SMEM((NBR, TB), i32),
             pltpu.SMEM((NBR, OWN_TB), i32),
+            pltpu.SMEM((1,), i32),
             pltpu.VMEM((HALF_CAP, FEAT), f32),
             pltpu.VMEM((GROUPS * 4, BLOCK, FEAT), bf16),
             pltpu.VMEM((GROUPS * 4, BLOCK, FEAT), bf16),
@@ -436,7 +442,7 @@
             pltpu.VMEM((OWN_TB, BLOCK, HID), f32),
             dma,
             dma,
-            dma((11,)),
+            dma((12,)),
             dma((CHUNKS,)),
             dma((CHUNKS,)),
             dma,
@@ -448,8 +454,8 @@
             dma((4,)),
             dma((4,)),
             dma((4,)),
-            dma((ROW_CHUNKS,)),
-            dma((ROW_CHUNKS,)),
+            dma((PARTS,)),
+            dma((PARTS,)),
         ],
         compiler_params=pltpu.CompilerParams(
             collective_id=0, has_side_effects=True, vmem_limit_bytes=58 * 2**20

time: 78.2 us -> 78.1 us (level)
  no operation moved by 1% of the time
where the time goes in v5:
time: 78.1 us; the launch traced here: 78 us
  Pallas kernels  75.7 us (97%)
  matrix products  1.6 us (2%)
    pallas_call x1, Pallas kernels, body(): pl.pallas_call(kernel, out_shape=pltpu.VMEM((OWN_TB * BLOCK, HID), bf16),...  75.7 us
    dot_general x1, matrix products, body(): jnp.dot(layer_two, classifier, preferred_element_type=f32) + bias_class  1.6 us

profile of v5, /device:TPU:1, one launch (start us, length us, event | category | flops | bytes accessed | tf_op | source)
XLA Modules:
  0.0 78.0 jit_solution(17955882984048698388)
XLA Ops:
  0.0 0.0 copy-start
  0.7 0.0 copy-start.1
  0.7 75.7 %graph_layers.1 = bf16[2048,256]{1,0:T(8,128)(2,1)S(1)} custom-call(bf16[64,16384]{1,0:T(8,128)(2,1)} %store_hbm.1, s32[64,512]{1,0:T(8,128)} %req_hbm.1, s32[8,64]{1,0:T(8,128)} %bitcast.6, bf16[64,64,512]{2,1,0:T(8,128)(2,1)} %values_hbm.1, s32[1]{0:T(128)S(6)} %copy.16.frontier_hbm, bf16[128,256]{1,0:T(8,128)(2,1)} %w_self_hbm.1, ...), custom_call_target="tpu_custom_call" | custom-call | tf_op jit(solution)/shard_map/graph_layers/pallas_call | solution.py:408
  76.4 0.0 copy-done
  76.4 0.0 copy-done.1
  76.4 1.6 %convolution_add_fusion = f32[2048,172]{0,1:T(8,128)} fusion(bf16[2048,256]{1,0:T(8,128)(2,1)S(1)} %graph_layers.1, bf16[256,172]{0,1:T(8,128)(2,1)S(1)} %copy-done, f32[172]{0:T(256)S(1)} %copy-done.1), kind=kOutput, calls=%fused_computation | convolution fusion | flops 180707328 | bytes 2546352 | tf_op jit(solution)/shard_map/dot_general | solution.py:479
Async XLA Ops:
  0.0 76.4 %copy-start = (bf16[256,172]{0,1:T(8,128)(2,1)S(1)}, bf16[256,172]{0,1:T(8,128)(2,1)}, u32[]{:S(2)}) copy-start(bf16[256,172]{0,1:T(8,128)(2,1)} %param.28) | copy-start | bytes 264196
  0.7 75.7 %copy-start.1 = (f32[172]{0:T(256)S(1)}, f32[172]{0:T(256)}, u32[]{:S(2)}) copy-start(f32[172]{0:T(256)} %param.29) | copy-start | bytes 2068

commit v6 on v5

--- a/solution.py
+++ b/solution.py
@@ -91,8 +91,8 @@
     bias_two,
     psend,
     precv,
-    totals,
-    totals_two,
+    inverse,
+    inverse_two,
     selfbuf,
     agg,
     l1,
@@ -243,8 +243,10 @@
     ones = jnp.ones((NBR * BLOCK, FEAT), bf16)
 
     def total(t, _):
-        totals[t] = jnp.dot(values[c * OWN_TB + t], ones, preferred_element_type=f32)
-        totals_two[t] = jnp.dot(values_two[t], ones, preferred_element_type=f32)
+        inverse[t] = 1.0 / jnp.dot(
+            values[c * OWN_TB + t], ones, preferred_element_type=f32
+        )
+        inverse_two[t] = 1.0 / jnp.dot(values_two[t], ones, preferred_element_type=f32)
         return 0
 
     lax.fori_loop(0, OWN_TB, total, 0)
@@ -340,7 +342,7 @@
         for j in range(m * 4 // PARTS, (m + 1) * 4 // PARTS):
             p_copy(j).wait_recv()
         part = pl.ds(m * PART_TB, PART_TB)
-        mean = ((agg[part] + precv[part]) / totals[part]).astype(bf16).reshape(PART_ROWS, FEAT)
+        mean = ((agg[part] + precv[part]) * inverse[part]).astype(bf16).reshape(PART_ROWS, FEAT)
         mine = selfbuf[pl.ds(m * 8 // PARTS, 8 // PARTS)].reshape(PART_ROWS, FEAT)
         both = jnp.concatenate([mine, mean], axis=1)
         pre = jnp.dot(both, w_first[...], preferred_element_type=f32) + bias[...]
@@ -367,8 +369,8 @@
             summed = jnp.dot(
                 values_two[t], jnp.concatenate(parts, axis=0), preferred_element_type=f32
             )
-            total = jnp.concatenate([totals_two[t], totals_two[t]], axis=1)
-            means.append((summed / total).astype(bf16))
+            total = jnp.concatenate([inverse_two[t], inverse_two[t]], axis=1)
+            means.append((summed * total).astype(bf16))
         mean = jnp.concatenate(means, axis=0)
         pre = (
             jnp.dot(mean, w_neigh_two[...], preferred_element_type=f32)

time: 78.1 us -> 78.1 us (level)
  no operation moved by 1% of the time
where the time goes in v6:
time: 78.1 us; the launch traced here: 78 us
  Pallas kernels  75.6 us (97%)
  matrix products  1.6 us (2%)
    pallas_call x1, Pallas kernels, body(): pl.pallas_call(kernel, out_shape=pltpu.VMEM((OWN_TB * BLOCK, HID), bf16),...  75.6 us
    dot_general x1, matrix products, body(): jnp.dot(layer_two, classifier, preferred_element_type=f32) + bias_class  1.6 us

profile of v6, /device:TPU:1, one launch (start us, length us, event | category | flops | bytes accessed | tf_op | source)
XLA Modules:
  0.0 78.0 jit_solution(11207115259499824676)
XLA Ops:
  0.0 0.0 copy-start
  0.7 0.0 copy-start.1
  0.7 75.6 %graph_layers.1 = bf16[2048,256]{1,0:T(8,128)(2,1)S(1)} custom-call(bf16[64,16384]{1,0:T(8,128)(2,1)} %store_hbm.1, s32[64,512]{1,0:T(8,128)} %req_hbm.1, s32[8,64]{1,0:T(8,128)} %bitcast.6, bf16[64,64,512]{2,1,0:T(8,128)(2,1)} %values_hbm.1, s32[1]{0:T(128)S(6)} %copy.16.frontier_hbm, bf16[128,256]{1,0:T(8,128)(2,1)} %w_self_hbm.1, ...), custom_call_target="tpu_custom_call" | custom-call | tf_op jit(solution)/shard_map/graph_layers/pallas_call | solution.py:410
  76.3 0.0 copy-done
  76.4 0.0 copy-done.1
  76.4 1.6 %convolution_add_fusion = f32[2048,172]{0,1:T(8,128)} fusion(bf16[2048,256]{1,0:T(8,128)(2,1)S(1)} %graph_layers.1, bf16[256,172]{0,1:T(8,128)(2,1)S(1)} %copy-done, f32[172]{0:T(256)S(1)} %copy-done.1), kind=kOutput, calls=%fused_computation | convolution fusion | flops 180707328 | bytes 2546352 | tf_op jit(solution)/shard_map/dot_general | solution.py:481
Async XLA Ops:
  0.0 76.3 %copy-start = (bf16[256,172]{0,1:T(8,128)(2,1)S(1)}, bf16[256,172]{0,1:T(8,128)(2,1)}, u32[]{:S(2)}) copy-start(bf16[256,172]{0,1:T(8,128)(2,1)} %param.28) | copy-start | bytes 264196
  0.7 75.7 %copy-start.1 = (f32[172]{0:T(256)S(1)}, f32[172]{0:T(256)}, u32[]{:S(2)}) copy-start(f32[172]{0:T(256)} %param.29) | copy-start | bytes 2068
